TPU v7x, 128 devices: a whole 4x4x4 slice. The times are simulated.
128 devices in a mesh: chan: 16 (over y, x), tm: 8 (over z, core).
Axes of the slice: x: 4, y: 4, z: 4, core: 2. Of those that a mesh axis runs over, the one named last changes fastest.
Arguments:
- samples: bfloat16 [256, 192, 4096], P('chan', 'tm'), may hold values from -6 to 6
- taps: float32 [16, 4096], replicated, may hold values from -1.5 to 1.5
- block_tile: int32 [120], replicated, may hold values from 0 to 15, as said below
- tile_slots: int32 [16], replicated, may hold values from 0 to 15, as said below
- kern_u: bfloat16 [16, 30720], replicated, may hold values from -1.1953125 to 1.1953125
- kern_v: bfloat16 [16, 30720], replicated, may hold values from -1.1953125 to 1.1953125
Outputs:
- uv_grid: float32 [16, 2048, 2, 256], P('tm', 'chan')
Inputs may be any that keep to these rules, and one draw needn't show every extreme that they name: `block_tile`: A tile's owner is (its position in tile_slots) // 2. The blocks that fall in the tiles of one owner are at most 30; in every draw one owner has exactly 30. `tile_slots`: each tile number stands once.
All inputs are finite; a program needn't handle non-finite values.
Results may differ from a plain program's by a relative error of at most 0.0077.
Values may be sent and summed in bfloat16 or wider, within the bound.
No kernel may reach another device: no remote copies, remote signals or barrier semaphores. Data moves between devices by JAX's collectives and lax.ppermute only.
A program may use at most 192 MiB of HBM per device.

v0:
```python
import math
import jax
import jax.numpy as jnp
import numpy as np
from jax import lax
from jax.sharding import PartitionSpec as P

SBLK = 16
GRID = 16


def passed_along(value, axis, steps):
    count = lax.axis_size(axis)
    leading, last = (max(0, -steps), min(count, count - steps))
    return lax.ppermute(value, axis, [(source, source + steps) for source in range(leading, last)])


def block_pairs(block_total):
    left_list = []
    right_list = []
    for p in range(block_total):
        for q in range(p + 1, block_total):
            left_list.append(p)
            right_list.append(q)
    return (np.array(left_list, dtype=np.int32), np.array(right_list, dtype=np.int32))


def make_kernel(u_part, v_part, block_total):
    u_cols = u_part.astype(jnp.float32).reshape(GRID, block_total, SBLK * SBLK).transpose(1, 2, 0)
    v_cols = v_part.astype(jnp.float32).reshape(GRID, block_total, SBLK * SBLK).transpose(1, 2, 0)
    product = u_cols[:, :, :, None] * v_cols[:, :, None, :]
    return product.reshape(block_total, SBLK * SBLK, GRID * GRID).astype(jnp.bfloat16)


def body(samples, taps, block_tile, tile_slots, kern_u, kern_v):
    station_count, frame_count, length = samples.shape
    channel_count = length // 2
    chan_size = lax.axis_size("chan")
    tm_size = lax.axis_size("tm")
    group_count = chan_size * tm_size
    group_width = channel_count // group_count
    tap_count = taps.shape[0]
    history = passed_along(samples[:, frame_count - (tap_count - 1) :], "tm", 1)
    padded = jnp.concatenate([history, samples], axis=1)
    filtered = jnp.zeros((station_count, frame_count, length), jnp.float32)
    for tap_index in range(tap_count):
        offset = tap_count - 1 - tap_index
        filtered = filtered + taps[tap_index] * padded[:, offset : offset + frame_count].astype(
            jnp.float32
        )
    rows_in = filtered.astype(jnp.bfloat16).reshape(station_count * frame_count, length)
    dft_scale = 1.0 / math.sqrt(length)
    block_cols = min(channel_count, 256)
    groups_per_block = block_cols // group_width
    positions = jnp.arange(length, dtype=jnp.int32)[:, None, None]
    pieces = []
    for column_block in range(channel_count // block_cols):
        channels = column_block * block_cols + jnp.arange(block_cols, dtype=jnp.int32).reshape(
            1, groups_per_block, group_width
        )
        phase_int = positions * channels % length
        phase_angle = phase_int.astype(jnp.float32) * (2.0 * math.pi / length)
        cosine = jnp.cos(phase_angle).astype(jnp.bfloat16)
        sine_neg = (-jnp.sin(phase_angle)).astype(jnp.bfloat16)
        dft_table = jnp.stack([cosine, sine_neg], axis=2).reshape(length, 2 * block_cols)
        spectrum = (
            lax.dot_general(
                dft_table, rows_in, (((0,), (1,)), ((), ())), preferred_element_type=jnp.float32
            )
            * dft_scale
        )
        pieces.append(
            spectrum.astype(jnp.bfloat16).reshape(
                groups_per_block, 2, group_width, station_count, frame_count
            )
        )
    spectra = jnp.concatenate(pieces, axis=0)
    stations = station_count * chan_size
    frames = frame_count * tm_size
    arranged = spectra.reshape(chan_size, tm_size, 2, group_width, station_count, frame_count)
    turned = lax.all_to_all(
        lax.all_to_all(arranged, "chan", split_axis=0, concat_axis=4, tiled=True),
        "tm",
        split_axis=1,
        concat_axis=5,
        tiled=True,
    )
    turned = turned.reshape(2, group_width, stations, frames)
    block_rows = stations // SBLK
    block_total = block_rows * (block_rows - 1) // 2
    vis_scale = 1.0 / math.sqrt(frames)
    swapped = jnp.stack([turned[1], -turned[0]], axis=0)
    real_part = (
        jnp.einsum("cgib,cgjb->gij", turned, turned, preferred_element_type=jnp.float32) * vis_scale
    )
    imag_part = (
        jnp.einsum("cgib,cgjb->gij", swapped, turned, preferred_element_type=jnp.float32)
        * vis_scale
    )
    left_idx, right_idx = block_pairs(block_rows)
    visibility = jnp.stack([real_part, imag_part], axis=1).reshape(
        group_width, 2, block_rows, SBLK, block_rows, SBLK
    )
    visibility = visibility[:, :, left_idx, :, right_idx, :]
    blocks = visibility.reshape(block_total, group_width, 2, SBLK * SBLK).astype(jnp.bfloat16)
    tile_count = tile_slots.shape[0]
    slot_ids = jnp.arange(tile_count, dtype=jnp.int32)
    tile_match = block_tile[:, None] == tile_slots[None, :]
    slot_of_block = jnp.sum(jnp.where(tile_match, slot_ids[None, :], 0), axis=1)
    kernel = make_kernel(kern_u, kern_v, block_total)
    per_block = jnp.einsum("mgce,mel->mgcl", blocks, kernel, preferred_element_type=jnp.float32)
    slot_hits = (slot_of_block[:, None] == slot_ids[None, :]).astype(jnp.float32)
    partial_value = jnp.einsum(
        "mgcl,ms->sgcl", per_block, slot_hits, precision=lax.Precision.HIGHEST
    )
    uv_grid = lax.all_to_all(partial_value, "tm", split_axis=0, concat_axis=1, tiled=True)
    return uv_grid


def solution(mesh):
    placed = (P("chan", "tm", None), P(), P(), P(), P(), P())
    return jax.shard_map(
        body, mesh=mesh, in_specs=placed, out_specs=P("tm", "chan", None, None), check_vma=False
    )
```

profile of v0, /device:TPU:1, one launch (start us, length us, event | category | flops | bytes accessed | tf_op | source)
XLA Modules:
  0.0 647.3 jit_solution(4451937538021533933)
XLA Ops:
  9.7 18.1 %cosine_convert_fusion.7 = (bf16[4096,16,1,16]{0,3,2,1:T(8,128)(2,1)S(1)}, bf16[4096,16,1,16]{0,3,2,1:T(8,128)(2,1)S(1)}) fusion(s32[16,16]{1,0:T(8,128)S(1)} %multiply_add_fusion), kind=kLoop, calls=%fused_computation.119 | loop fusion | flops 17825792 | bytes 4195328 | tf_op jit(solution)/shard_map/convert_element_type | solution.py:63
  27.7 18.1 %cosine_convert_fusion.6 = (bf16[4096,16,1,16]{0,3,2,1:T(8,128)(2,1)S(1)}, bf16[4096,16,1,16]{0,3,2,1:T(8,128)(2,1)S(1)}) fusion(s32[16,16]{1,0:T(8,128)S(1)} %fusion.84), kind=kLoop, calls=%fused_computation.115 | loop fusion | flops 17825792 | bytes 4195328 | tf_op jit(solution)/shard_map/convert_element_type | solution.py:63
  45.8 18.1 %cosine_convert_fusion.5 = (bf16[4096,16,1,16]{0,3,2,1:T(8,128)(2,1)S(1)}, bf16[4096,16,1,16]{0,3,2,1:T(8,128)(2,1)S(1)}) fusion(s32[16,16]{1,0:T(8,128)S(1)} %fusion.83), kind=kLoop, calls=%fused_computation.111 | loop fusion | flops 17825792 | bytes 4195328 | tf_op jit(solution)/shard_map/convert_element_type | solution.py:63
  63.9 18.1 %cosine_convert_fusion.4 = (bf16[4096,16,1,16]{0,3,2,1:T(8,128)(2,1)S(1)}, bf16[4096,16,1,16]{0,3,2,1:T(8,128)(2,1)S(1)}) fusion(s32[16,16]{1,0:T(8,128)S(1)} %fusion.82), kind=kLoop, calls=%fused_computation.107 | loop fusion | flops 17825792 | bytes 4195328 | tf_op jit(solution)/shard_map/convert_element_type | solution.py:63
  82.0 18.1 %cosine_convert_fusion.3 = (bf16[4096,16,1,16]{0,3,2,1:T(8,128)(2,1)S(1)}, bf16[4096,16,1,16]{0,3,2,1:T(8,128)(2,1)S(1)}) fusion(s32[16,16]{1,0:T(8,128)S(1)} %fusion.81), kind=kLoop, calls=%fused_computation.103 | loop fusion | flops 17825792 | bytes 4195328 | tf_op jit(solution)/shard_map/convert_element_type | solution.py:63
  100.0 18.1 %cosine_convert_fusion.2 = (bf16[4096,16,1,16]{0,3,2,1:T(8,128)(2,1)S(1)}, bf16[4096,16,1,16]{0,3,2,1:T(8,128)(2,1)S(1)}) fusion(s32[16,16]{1,0:T(8,128)S(1)} %fusion.80), kind=kLoop, calls=%fused_computation.99 | loop fusion | flops 17825792 | bytes 4195328 | tf_op jit(solution)/shard_map/convert_element_type | solution.py:63
  118.1 18.1 %cosine_convert_fusion.1 = (bf16[4096,16,1,16]{0,3,2,1:T(8,128)(2,1)S(1)}, bf16[4096,16,1,16]{0,3,2,1:T(8,128)(2,1)S(1)}) fusion(s32[16,16]{1,0:T(8,128)S(1)} %fusion.79), kind=kLoop, calls=%fused_computation.95 | loop fusion | flops 17825792 | bytes 4195328 | tf_op jit(solution)/shard_map/convert_element_type | solution.py:63
  136.2 19.0 %cosine_convert_fusion = (bf16[4096,16,1,16]{0,3,2,1:T(8,128)(2,1)S(1)}, bf16[4096,16,1,16]{0,3,2,1:T(8,128)(2,1)}) fusion(s32[16,16]{1,0:T(8,128)S(1)} %fusion.78), kind=kLoop, calls=%fused_computation.91 | loop fusion | flops 17825792 | bytes 4195328 | tf_op jit(solution)/shard_map/convert_element_type | solution.py:63
  178.3 23.2 %add_convert_fusion = bf16[16,24,4096]{2,1,0:T(8,128)(2,1)} fusion(bf16[16,24,4096]{2,1,0:T(8,128)(2,1)S(1)} %copy-done, bf16[16,15,4096]{2,1,0:T(8,128)(2,1)} %copy.81, f32[4096]{0:T(1024)S(1)} %bitcast.136, f32[4096]{0:T(1024)S(1)} %bitcast.137, f32[4096]{0:T(1024)S(1)} %bitcast.123, f32[4096]{0:T(1024)S(1)} %bitcast.124, f32[4096]{0:T(1024)S(1)} %bitcast.125, ...), kind=kLoop, calls=%fused_computation.52 | loop fusion | flops 146276352 | bytes 8519680 | tf_op jit(solution)/shard_map/convert_element_type | solution.py:51
  288.1 22.6 %reshape.779 = bf16[16,2,49152]{2,1,0:T(2,128)(2,1)S(1)} reshape(bf16[16,8,2,16,16,24]{5,4,3,2,1,0:T(8,128)(2,1)} %bitcast.96) | data formatting | bytes 6291456
  310.7 47.5 %all_to_all.51 = bf16[16,2,49152]{2,1,0:T(2,128)(2,1)} all-to-all(bf16[16,2,49152]{2,1,0:T(2,128)(2,1)S(1)} %reshape.779), channel_id=1, replica_groups=mesh['chan'=16,'tm'=8] {'chan'}, dimensions={0} | all-to-all | bytes 6291456 | tf_op jit(solution)/shard_map/all_to_all | solution.py:82
  358.2 25.0 %reshape.780 = bf16[16,8,2,16,16,24]{5,4,3,2,1,0:T(8,128)(2,1)} reshape(bf16[16,2,49152]{2,1,0:T(2,128)(2,1)} %all_to_all.51) | data formatting | bytes 6291456
  383.2 32.4 %copy.82 = bf16[1,8,2,16,16,16,24]{5,4,6,3,2,1,0:T(8,128)(2,1)} copy(bf16[1,8,2,16,16,16,24]{6,5,3,2,1,4,0:T(8,128)(2,1)} %bitcast.92) | data formatting | bytes 6291456 | tf_op jit(solution)/shard_map/all_to_all | solution.py:82
  415.6 30.1 %all_to_all.40 = bf16[1,8,2,16,256,24]{4,5,3,2,1,0:T(8,128)(2,1)} reshape(bf16[1,8,2,16,16,16,24]{5,4,6,3,2,1,0:T(8,128)(2,1)} %copy.82) | data formatting | bytes 6291456 | tf_op jit(solution)/shard_map/all_to_all | solution.py:82
  462.2 25.4 %all-to-all-done.1 = bf16[1,8,2,16,256,24]{4,5,3,2,0,1:T(8,128)(2,1)S(1)} async-done(((bf16[1,8,2,16,256,24]{4,5,3,2,0,1:T(8,128)(2,1)}), bf16[1,8,2,16,256,24]{4,5,3,2,0,1:T(8,128)(2,1)S(1)}, u32[]{:S(2)}, u32[]{:S(2)}) %all-to-all-start.1) | async-done | bytes 3145760 | tf_op jit(solution)/shard_map/all_to_all | solution.py:81
  492.8 17.4 %stack.63 = bf16[16,1,16,16,16,16]{5,4,3,2,0,1:T(8,128)(2,1)} reshape(bf16[16,256,256]{2,1,0:T(8,128)(2,1)} %bitcast_multiply_fusion) | data formatting | bytes 4194304 | tf_op jit(solution)/shard_map/stack | solution.py:101
  510.2 16.6 %copy.88 = bf16[16,1,16,16,16,16]{5,3,4,2,1,0:T(8,128)(2,1)} copy(bf16[16,1,16,16,16,16]{5,4,3,2,0,1:T(8,128)(2,1)} %stack.63) | data formatting | bytes 4194304 | tf_op jit(solution)/shard_map/stack | solution.py:101
  526.9 14.3 %stack.61 = bf16[16,1,16,16,16,16]{5,4,3,2,0,1:T(8,128)(2,1)} reshape(bf16[16,256,256]{2,1,0:T(8,128)(2,1)S(1)} %bitcast_multiply_fusion.1) | data formatting | bytes 4194304 | tf_op jit(solution)/shard_map/stack | solution.py:101
  541.2 16.6 %copy.87 = bf16[16,1,16,16,16,16]{5,3,4,2,1,0:T(8,128)(2,1)} copy(bf16[16,1,16,16,16,16]{5,4,3,2,0,1:T(8,128)(2,1)} %stack.61) | data formatting | bytes 4194304 | tf_op jit(solution)/shard_map/stack | solution.py:101
  557.8 22.7 %pad_maximum_fusion = bf16[16,2,16,16,16,16]{5,3,4,2,1,0:T(8,128)(2,1)} fusion(bf16[16,1,16,16,16,16]{5,3,4,2,1,0:T(8,128)(2,1)} %copy.88, bf16[16,1,16,16,16,16]{5,3,4,2,1,0:T(8,128)(2,1)} %copy.87), kind=kLoop, calls=%fused_computation.1 | loop fusion | flops 2097152 | bytes 8388608 | tf_op jit(solution)/shard_map/stack | solution.py:101
  580.5 12.2 %gather_fusion = bf16[120,16,2,16,16]{4,3,2,1,0:T(8,128)(2,1)} fusion(bf16[16,2,16,16,16,16]{5,3,4,2,1,0:T(8,128)(2,1)} %pad_maximum_fusion, s32[120]{0:T(128)S(1)} %copy-done.8), kind=kCustom, calls=%fused_computation | custom fusion | bytes 3933120 | tf_op jit(solution)/shard_map/gather | solution.py:104
  592.7 18.3 %copy.89 = bf16[120,16,2,16,16]{0,4,3,2,1:T(8,128)(2,1)S(1)} copy(bf16[120,16,2,16,16]{4,3,2,1,0:T(8,128)(2,1)} %gather_fusion) | data formatting | bytes 3932160 | tf_op jit(solution)/shard_map/gather | solution.py:104
  614.3 12.6 %fusion.91 = f32[120,16,2,256]{3,1,2,0:T(8,128)} fusion(bf16[120,16,2,256]{3,1,2,0:T(8,128)(2,1)} %copy.92, bf16[120,256,256,1]{1,2,3,0:T(8,128)(2,1)} %bitcast.93), kind=kOutput, calls=%fused_computation.193 | convolution fusion | flops 503316480 | bytes 21626880 | tf_op jit(solution)/shard_map/mgce,mel->mgcl/dot_general | solution.py:111
  633.2 12.6 %all_to_all.52 = f32[16,16,2,256]{3,2,1,0:T(2,128)S(1)} all-to-all(f32[16,16,2,256]{3,2,1,0:T(2,128)S(1)} %copy.95), channel_id=1, replica_groups=mesh['chan'=16,'tm'=8] {'tm'}, dimensions={0} | all-to-all | bytes 1048576 | tf_op jit(solution)/shard_map/all_to_all | solution.py:116
  (88 shorter events, 151.3 us)
Async XLA Ops:
  4.6 169.6 %collective-permute-start = (bf16[16,15,4096]{2,0,1:T(8,128)(2,1)}, bf16[16,15,4096]{2,0,1:T(8,128)(2,1)}, u32[]{:S(2)}, u32[]{:S(2)}) collective-permute-start(bf16[16,15,4096]{2,0,1:T(8,128)(2,1)} %copy.103), channel_id=1, source_target_pairs={{0,1},{1,2},{2,3},{3,4},{4,5},{5,6},{6,7},{8,9},{9,10},{10,11},{11... | collective-permute-start | bytes 5898248 | tf_op jit(solution)/shard_map/ppermute | solution.py:15
  169.3 2.3 copy-start.7
  171.6 2.4 copy-start.10
  174.0 4.4 copy-start
  209.8 2.9 copy-start.9
  275.6 2.2 copy-start.1
  275.6 3.9 copy-start.2
  277.8 3.4 copy-start.3
  279.5 3.5 copy-start.4
  281.2 3.5 copy-start.5
  283.0 3.4 copy-start.6
  445.7 42.0 %all-to-all-start.1 = ((bf16[1,8,2,16,256,24]{4,5,3,2,0,1:T(8,128)(2,1)}), bf16[1,8,2,16,256,24]{4,5,3,2,0,1:T(8,128)(2,1)S(1)}, u32[]{:S(2)}, u32[]{:S(2)}) async-start(bf16[1,8,2,16,256,24]{4,5,3,2,0,1:T(8,128)(2,1)} %bitcast.97), calls=%async_computation.1 | async-start | bytes 6291456 | tf_op jit(solution)/shard_map/all_to_all | solution.py:81
  450.1 2.7 copy-start.11
  450.1 2.7 copy-start.12
  557.8 22.7 %copy-start.8 = (s32[120]{0:T(128)S(1)}, s32[120]{0:T(128)}, u32[]{:S(2)}) copy-start(s32[120]{0:T(128)} %constant.106) | copy-start | bytes 1444
where the time goes:
time: 658 us; the launch traced here: 647 us
  local copies, waits for them, and re-layouts  264 us (40%)
  other arithmetic  222 us (34%)
  matrix products  65.5 us (10%)
  blocking collectives  60.1 us (9%)
  waiting for transfers between devices  25.4 us (4%)
  starting transfers between devices  9.37 us (1%)
    convert_element_type x8, other arithmetic, body(): cosine = jnp.cos(phase_angle).astype(jnp.bfloat16)  145 us
    another operation x4, local copies, waits for them, and re-layouts, body(): jnp.stack([real_part, imag_part], axis=1)  65 us
    unnamed x36, local copies, waits for them, and re-layouts  63.9 us
    all_to_all x2, local copies, waits for them, and re-layouts, body(): lax.all_to_all(arranged, 'chan', split_axis=0, concat_axis=4, tiled=True)  62.5 us
    all_to_all x1, blocking collectives, body(): lax.all_to_all(arranged, 'chan', split_axis=0, concat_axis=4, tiled=True)  47.5 us
    dot_general x8, matrix products, body(): lax.dot_general(dft_table, rows_in, (((0,), (1,)), ((), ())), preferred_e...  42.9 us
    gather x2, local copies, waits for them, and re-layouts, body(): visibility = visibility[:, :, left_idx, :, right_idx, :]  30.6 us
    reshape x8, local copies, waits for them, and re-layouts, body(): spectrum.astype(jnp.bfloat16)  28.2 us
  transfers between devices with their start and end apart: 2, of which 1 were waited for; matrix products, arithmetic and copies ran while one was open for 27% of the time, Pallas kernels for 0%

commit v1 on v0

--- a/solution.py
+++ b/solution.py
@@ -4,6 +4,7 @@
 import numpy as np
 from jax import lax
 from jax.sharding import PartitionSpec as P
+from jax.lax import axis_index, ppermute, psum
 
 SBLK = 16
 GRID = 16
@@ -113,7 +114,14 @@
     partial_value = jnp.einsum(
         "mgcl,ms->sgcl", per_block, slot_hits, precision=lax.Precision.HIGHEST
     )
-    uv_grid = lax.all_to_all(partial_value, "tm", split_axis=0, concat_axis=1, tiled=True)
+    p_next, kept_arr = (psum(1, "tm"), axis_index("tm"))
+    back = partial_value.shape[0] // p_next
+    frame_out = jnp.roll(partial_value, -kept_arr * back, 0)
+    rack = [lax.slice_in_dim(frame_out, 0, back, axis=0)]
+    for c in range(1, p_next):
+        arr_next = lax.slice_in_dim(frame_out, c * back, (c + 1) * back, axis=0)
+        rack.append(ppermute(arr_next, "tm", [(jj, (jj + c) % p_next) for jj in range(p_next)]))
+    uv_grid = jnp.roll(jnp.concatenate(rack[::-1], 1), (kept_arr + 1) * rack[0].shape[1], 1)
     return uv_grid
 
 

time: 658 us -> 658 us (level)
  blocking collectives: 60.1 us -> 47.4 us
  starting transfers between devices: 9.37 us -> 16.7 us
    all_to_all x1 -> x0, blocking collectives: 12.6 us -> none  [body(): lax.all_to_all(partial_value, 'tm', split_axis=0, concat_axis=1, tiled=True)]
    ppermute x0 -> x7, starting transfers between devices: none -> 7.31 us  [body(): ppermute(arr_next, 'tm', [(jj, (jj + c) % p_next) for jj in range(p_next)])]
    unnamed x36 -> x51, local copies, waits for them, and re-layouts: 63.9 us -> 64.1 us
  transfers between devices with their start and end apart: 2 -> 9, of which waited for: 1 -> 4; matrix products, arithmetic and copies ran while one was open for 27% -> 28% of each run, Pallas kernels for 0% -> 0%
where the time goes in v1:
time: 658 us; the launch traced here: 647 us
  local copies, waits for them, and re-layouts  267 us (41%)
  other arithmetic  225 us (34%)
  matrix products  65.5 us (10%)
  blocking collectives  47.4 us (7%)
  waiting for transfers between devices  25.4 us (4%)
  starting transfers between devices  16.7 us (3%)
    convert_element_type x8, other arithmetic, body(): cosine = jnp.cos(phase_angle).astype(jnp.bfloat16)  145 us
    another operation x4, local copies, waits for them, and re-layouts, body(): jnp.stack([real_part, imag_part], axis=1)  65.1 us
    unnamed x51, local copies, waits for them, and re-layouts  64.1 us
    all_to_all x2, local copies, waits for them, and re-layouts, body(): lax.all_to_all(arranged, 'chan', split_axis=0, concat_axis=4, tiled=True)  62.5 us
    all_to_all x1, blocking collectives, body(): lax.all_to_all(arranged, 'chan', split_axis=0, concat_axis=4, tiled=True)  47.4 us
    dot_general x8, matrix products, body(): lax.dot_general(dft_table, rows_in, (((0,), (1,)), ((), ())), preferred_e...  42.9 us
    gather x2, local copies, waits for them, and re-layouts, body(): visibility = visibility[:, :, left_idx, :, right_idx, :]  30.6 us
    reshape x8, local copies, waits for them, and re-layouts, body(): spectrum.astype(jnp.bfloat16)  28.2 us
  transfers between devices with their start and end apart: 9, of which 4 were waited for; matrix products, arithmetic and copies ran while one was open for 28% of the time, Pallas kernels for 0%

profile of v1, /device:TPU:1, one launch (start us, length us, event | category | flops | bytes accessed | tf_op | source)
XLA Modules:
  0.0 647.0 jit_solution(8940418722391289883)
XLA Ops:
  9.6 18.1 %cosine_convert_fusion.7 = (bf16[4096,16,1,16]{0,3,2,1:T(8,128)(2,1)S(1)}, bf16[4096,16,1,16]{0,3,2,1:T(8,128)(2,1)S(1)}) fusion(s32[16,16]{1,0:T(8,128)S(1)} %multiply_add_fusion), kind=kLoop, calls=%fused_computation.119 | loop fusion | flops 17825792 | bytes 4195328 | tf_op jit(solution)/shard_map/convert_element_type | solution.py:64
  27.7 18.1 %cosine_convert_fusion.6 = (bf16[4096,16,1,16]{0,3,2,1:T(8,128)(2,1)S(1)}, bf16[4096,16,1,16]{0,3,2,1:T(8,128)(2,1)S(1)}) fusion(s32[16,16]{1,0:T(8,128)S(1)} %fusion.85), kind=kLoop, calls=%fused_computation.115 | loop fusion | flops 17825792 | bytes 4195328 | tf_op jit(solution)/shard_map/convert_element_type | solution.py:64
  45.8 18.1 %cosine_convert_fusion.5 = (bf16[4096,16,1,16]{0,3,2,1:T(8,128)(2,1)S(1)}, bf16[4096,16,1,16]{0,3,2,1:T(8,128)(2,1)S(1)}) fusion(s32[16,16]{1,0:T(8,128)S(1)} %fusion.84), kind=kLoop, calls=%fused_computation.111 | loop fusion | flops 17825792 | bytes 4195328 | tf_op jit(solution)/shard_map/convert_element_type | solution.py:64
  63.9 18.1 %cosine_convert_fusion.4 = (bf16[4096,16,1,16]{0,3,2,1:T(8,128)(2,1)S(1)}, bf16[4096,16,1,16]{0,3,2,1:T(8,128)(2,1)S(1)}) fusion(s32[16,16]{1,0:T(8,128)S(1)} %fusion.83), kind=kLoop, calls=%fused_computation.107 | loop fusion | flops 17825792 | bytes 4195328 | tf_op jit(solution)/shard_map/convert_element_type | solution.py:64
  81.9 18.1 %cosine_convert_fusion.3 = (bf16[4096,16,1,16]{0,3,2,1:T(8,128)(2,1)S(1)}, bf16[4096,16,1,16]{0,3,2,1:T(8,128)(2,1)S(1)}) fusion(s32[16,16]{1,0:T(8,128)S(1)} %fusion.82), kind=kLoop, calls=%fused_computation.103 | loop fusion | flops 17825792 | bytes 4195328 | tf_op jit(solution)/shard_map/convert_element_type | solution.py:64
  100.0 18.1 %cosine_convert_fusion.2 = (bf16[4096,16,1,16]{0,3,2,1:T(8,128)(2,1)S(1)}, bf16[4096,16,1,16]{0,3,2,1:T(8,128)(2,1)S(1)}) fusion(s32[16,16]{1,0:T(8,128)S(1)} %fusion.81), kind=kLoop, calls=%fused_computation.99 | loop fusion | flops 17825792 | bytes 4195328 | tf_op jit(solution)/shard_map/convert_element_type | solution.py:64
  118.1 18.1 %cosine_convert_fusion.1 = (bf16[4096,16,1,16]{0,3,2,1:T(8,128)(2,1)S(1)}, bf16[4096,16,1,16]{0,3,2,1:T(8,128)(2,1)S(1)}) fusion(s32[16,16]{1,0:T(8,128)S(1)} %fusion.80), kind=kLoop, calls=%fused_computation.95 | loop fusion | flops 17825792 | bytes 4195328 | tf_op jit(solution)/shard_map/convert_element_type | solution.py:64
  136.2 19.0 %cosine_convert_fusion = (bf16[4096,16,1,16]{0,3,2,1:T(8,128)(2,1)S(1)}, bf16[4096,16,1,16]{0,3,2,1:T(8,128)(2,1)}) fusion(s32[16,16]{1,0:T(8,128)S(1)} %fusion.79), kind=kLoop, calls=%fused_computation.91 | loop fusion | flops 17825792 | bytes 4195328 | tf_op jit(solution)/shard_map/convert_element_type | solution.py:64
  178.4 23.2 %add_convert_fusion = bf16[16,24,4096]{2,1,0:T(8,128)(2,1)} fusion(bf16[16,24,4096]{2,1,0:T(8,128)(2,1)S(1)} %copy-done, bf16[16,15,4096]{2,1,0:T(8,128)(2,1)} %copy.79, f32[4096]{0:T(1024)S(1)} %bitcast.131, f32[4096]{0:T(1024)S(1)} %bitcast.132, f32[4096]{0:T(1024)S(1)} %bitcast.118, f32[4096]{0:T(1024)S(1)} %bitcast.119, f32[4096]{0:T(1024)S(1)} %bitcast.120, ...), kind=kLoop, calls=%fused_computation.52 | loop fusion | flops 146276352 | bytes 8519680 | tf_op jit(solution)/shard_map/convert_element_type | solution.py:52
  288.2 22.6 %reshape.779 = bf16[16,2,49152]{2,1,0:T(2,128)(2,1)S(1)} reshape(bf16[16,8,2,16,16,24]{5,4,3,2,1,0:T(8,128)(2,1)} %bitcast.92) | data formatting | bytes 6291456
  310.9 47.4 %all_to_all.33 = bf16[16,2,49152]{2,1,0:T(2,128)(2,1)} all-to-all(bf16[16,2,49152]{2,1,0:T(2,128)(2,1)S(1)} %reshape.779), channel_id=1, replica_groups=mesh['chan'=16,'tm'=8] {'chan'}, dimensions={0} | all-to-all | bytes 6291456 | tf_op jit(solution)/shard_map/all_to_all | solution.py:83
  358.3 25.0 %reshape.780 = bf16[16,8,2,16,16,24]{5,4,3,2,1,0:T(8,128)(2,1)} reshape(bf16[16,2,49152]{2,1,0:T(2,128)(2,1)} %all_to_all.33) | data formatting | bytes 6291456
  383.3 32.4 %copy.80 = bf16[1,8,2,16,16,16,24]{5,4,6,3,2,1,0:T(8,128)(2,1)} copy(bf16[1,8,2,16,16,16,24]{6,5,3,2,1,4,0:T(8,128)(2,1)} %bitcast.88) | data formatting | bytes 6291456 | tf_op jit(solution)/shard_map/all_to_all | solution.py:83
  415.7 30.1 %all_to_all.27 = bf16[1,8,2,16,256,24]{4,5,3,2,1,0:T(8,128)(2,1)} reshape(bf16[1,8,2,16,16,16,24]{5,4,6,3,2,1,0:T(8,128)(2,1)} %copy.80) | data formatting | bytes 6291456 | tf_op jit(solution)/shard_map/all_to_all | solution.py:83
  458.2 8.6 %multiply_convert_fusion = bf16[120,256,16,16]{1,3,2,0:T(8,128)(2,1)} fusion(f32[120,256,16]{1,2,0:T(8,128)S(1)} %get-tuple-element.46, f32[120,256,16]{1,2,0:T(8,128)S(1)} %get-tuple-element.47), kind=kLoop, calls=%fused_computation.2 | loop fusion | flops 15728640 | bytes 19660800 | tf_op jit(solution)/shard_map/convert_element_type | solution.py:33
  466.9 20.9 %all-to-all-done.1 = bf16[1,8,2,16,256,24]{4,5,3,2,0,1:T(8,128)(2,1)S(1)} async-done(((bf16[1,8,2,16,256,24]{4,5,3,2,0,1:T(8,128)(2,1)}), bf16[1,8,2,16,256,24]{4,5,3,2,0,1:T(8,128)(2,1)S(1)}, u32[]{:S(2)}, u32[]{:S(2)}) %all-to-all-start.1) | async-done | bytes 3145760 | tf_op jit(solution)/shard_map/all_to_all | solution.py:82
  492.9 17.5 %stack.63 = bf16[16,1,16,16,16,16]{5,4,3,2,0,1:T(8,128)(2,1)} reshape(bf16[16,256,256]{2,1,0:T(8,128)(2,1)} %bitcast_multiply_fusion) | data formatting | bytes 4194304 | tf_op jit(solution)/shard_map/stack | solution.py:102
  510.3 16.6 %copy.86 = bf16[16,1,16,16,16,16]{5,3,4,2,1,0:T(8,128)(2,1)} copy(bf16[16,1,16,16,16,16]{5,4,3,2,0,1:T(8,128)(2,1)} %stack.63) | data formatting | bytes 4194304 | tf_op jit(solution)/shard_map/stack | solution.py:102
  527.0 14.4 %stack.61 = bf16[16,1,16,16,16,16]{5,4,3,2,0,1:T(8,128)(2,1)} reshape(bf16[16,256,256]{2,1,0:T(8,128)(2,1)S(1)} %bitcast_multiply_fusion.1) | data formatting | bytes 4194304 | tf_op jit(solution)/shard_map/stack | solution.py:102
  541.4 16.6 %copy.85 = bf16[16,1,16,16,16,16]{5,3,4,2,1,0:T(8,128)(2,1)} copy(bf16[16,1,16,16,16,16]{5,4,3,2,0,1:T(8,128)(2,1)} %stack.61) | data formatting | bytes 4194304 | tf_op jit(solution)/shard_map/stack | solution.py:102
  558.0 22.7 %pad_maximum_fusion = bf16[16,2,16,16,16,16]{5,3,4,2,1,0:T(8,128)(2,1)} fusion(bf16[16,1,16,16,16,16]{5,3,4,2,1,0:T(8,128)(2,1)} %copy.86, bf16[16,1,16,16,16,16]{5,3,4,2,1,0:T(8,128)(2,1)} %copy.85), kind=kLoop, calls=%fused_computation.1 | loop fusion | flops 2097152 | bytes 8388608 | tf_op jit(solution)/shard_map/stack | solution.py:102
  580.7 12.2 %gather_fusion = bf16[120,16,2,16,16]{4,3,2,1,0:T(8,128)(2,1)} fusion(bf16[16,2,16,16,16,16]{5,3,4,2,1,0:T(8,128)(2,1)} %pad_maximum_fusion, s32[120]{0:T(128)S(1)} %copy-done.8), kind=kCustom, calls=%fused_computation | custom fusion | bytes 3933120 | tf_op jit(solution)/shard_map/gather | solution.py:105
  592.9 18.3 %copy.87 = bf16[120,16,2,16,16]{0,4,3,2,1:T(8,128)(2,1)S(1)} copy(bf16[120,16,2,16,16]{4,3,2,1,0:T(8,128)(2,1)} %gather_fusion) | data formatting | bytes 3932160 | tf_op jit(solution)/shard_map/gather | solution.py:105
  614.5 12.6 %fusion.93 = f32[120,16,2,256]{3,1,2,0:T(8,128)} fusion(bf16[120,16,2,256]{3,1,2,0:T(8,128)(2,1)} %copy.90, bf16[120,256,256,1]{1,2,3,0:T(8,128)(2,1)} %bitcast.89), kind=kOutput, calls=%fused_computation.214 | convolution fusion | flops 503316480 | bytes 21626880 | tf_op jit(solution)/shard_map/mgce,mel->mgcl/dot_general | solution.py:112
  (119 shorter events, 159.4 us)
Async XLA Ops:
  4.6 169.7 %collective-permute-start = (bf16[16,15,4096]{2,0,1:T(8,128)(2,1)}, bf16[16,15,4096]{2,0,1:T(8,128)(2,1)}, u32[]{:S(2)}, u32[]{:S(2)}) collective-permute-start(bf16[16,15,4096]{2,0,1:T(8,128)(2,1)} %copy.100), channel_id=1, source_target_pairs={{0,1},{1,2},{2,3},{3,4},{4,5},{5,6},{6,7},{8,9},{9,10},{10,11},{11... | collective-permute-start | bytes 5898248 | tf_op jit(solution)/shard_map/ppermute | solution.py:16
  169.3 2.3 copy-start.7
  171.7 2.4 copy-start.10
  174.0 4.4 copy-start
  209.9 2.9 copy-start.9
  275.7 2.2 copy-start.1
  275.7 3.9 copy-start.2
  277.9 3.5 copy-start.3
  279.7 3.5 copy-start.4
  281.4 3.5 copy-start.5
  283.1 3.4 copy-start.6
  445.8 42.0 %all-to-all-start.1 = ((bf16[1,8,2,16,256,24]{4,5,3,2,0,1:T(8,128)(2,1)}), bf16[1,8,2,16,256,24]{4,5,3,2,0,1:T(8,128)(2,1)S(1)}, u32[]{:S(2)}, u32[]{:S(2)}) async-start(bf16[1,8,2,16,256,24]{4,5,3,2,0,1:T(8,128)(2,1)} %bitcast.93), calls=%async_computation.1 | async-start | bytes 6291456 | tf_op jit(solution)/shard_map/all_to_all | solution.py:82
  450.2 5.3 copy-start.11
  450.2 5.3 copy-start.12
  558.0 22.7 %copy-start.8 = (s32[120]{0:T(128)S(1)}, s32[120]{0:T(128)}, u32[]{:S(2)}) copy-start(s32[120]{0:T(128)} %constant.154) | copy-start | bytes 1444
  633.3 6.5 %collective-permute-start.1 = (f32[2,16,2,256]{3,0,2,1:T(2,128)S(1)}, f32[2,16,2,256]{3,0,2,1:T(2,128)S(1)}, u32[]{:S(2)}, u32[]{:S(2)}) collective-permute-start(f32[2,16,2,256]{3,0,2,1:T(2,128)S(1)} %get-tuple-element.13), channel_id=1, source_target_pairs={{0,7},{1,0},{2,1},{3,2},{4,3},{5,4},{6,5},{7,6},{8,15},{9,8},{10,9... | collective-permute-start | bytes 196616 | tf_op jit(solution)/shard_map/ppermute | solution.py:123
  634.1 5.6 collective-permute-start.2
  635.0 5.6 collective-permute-start.3
  636.2 4.7 collective-permute-start.4
  638.0 5.8 collective-permute-start.5
  639.8 5.3 collective-permute-start.6
  639.8 5.3 collective-permute-start.7
